TPU v7x, 32 devices: a whole 2x2x4 slice. The times are simulated.
32 devices in a mesh: tm: 4 (over y, x), rows: 4 (over z), cols: 2 (over core).
Axes of the slice: x: 2, y: 2, z: 4, core: 2. Of those that a mesh axis runs over, the one named last changes fastest.
Arguments:
- latent_video: bfloat16 [24, 128, 64, 128], P('tm', 'rows', 'cols'), may hold values from -6 to 6
- input_kernel: bfloat16 [3, 3, 128, 256], replicated, may hold values from -0.1875 to 0.1875
- output_kernel: bfloat16 [3, 3, 256, 128], replicated, may hold values from -0.125 to 0.125
- decay_rate: float32 [24, 256], P('tm'), may hold values from 0.4 to 0.999, as said below
- skip_gain: float32 [128], replicated, may hold values from 0.25 to 1.75
Outputs:
- layer_output: bfloat16 [24, 128, 64, 128], P('tm', 'rows', 'cols')
Inputs may be any that keep to these rules, and one draw needn't show every extreme that they name: `decay_rate`: every decay factor lies strictly between zero and one.
All inputs are finite; a program needn't handle non-finite values.
Results may differ from a plain program's by a relative error of at most 0.0048.
Values may be sent and summed in bfloat16 or wider, within the bound.
A program may use at most 128 MiB of HBM per device.

v0:
```python
import jax
import jax.numpy as jnp
from jax import lax
from jax.sharding import PartitionSpec as P


def with_halo(block, sides, width):
    for axis, dim in sides:
        count = lax.axis_size(axis)
        forward = [(i, i + 1) for i in range(count - 1)]
        backward = [(target, source) for source, target in forward]
        low = lax.ppermute(
            lax.slice_in_dim(block, block.shape[dim] - width, None, axis=dim), axis, forward
        )
        high = lax.ppermute(lax.slice_in_dim(block, 0, width, axis=dim), axis, backward)
        block = jnp.concatenate([low, block, high], axis=dim)
    return block


def stencil(field, kernel):
    height = field.shape[1] - 2
    width = field.shape[2] - 2
    summed = jnp.zeros((field.shape[0], height, width, kernel.shape[3]), jnp.float32)
    for row_off in range(3):
        for col_off in range(3):
            window = field[:, row_off : row_off + height, col_off : col_off + width, :]
            summed = summed + jnp.einsum(
                "fhwc,cs->fhws",
                window,
                kernel[row_off, col_off],
                preferred_element_type=jnp.float32,
            )
    return summed


def advance(carried, inputs):
    running, product = carried
    drive_now, rate_now = inputs
    running = rate_now * running + drive_now
    product = product * rate_now
    return ((running, product), (running, product))


def on_device(latent_video, input_kernel, output_kernel, decay_rate, skip_gain):
    padded = with_halo(latent_video, (("rows", 1), ("cols", 2)), 1)
    drive = stencil(padded, input_kernel)
    start = (jnp.zeros(drive.shape[1:], jnp.float32), jnp.ones(decay_rate.shape[1:], jnp.float32))
    finals, history = lax.scan(advance, start, (drive, decay_rate))
    local_states, products = history
    local_end, block_decay = finals
    decay_table = lax.all_gather(block_decay[None, :], "tm", axis=0, tiled=True)
    count = decay_table.shape[0]
    own_index = lax.axis_index("tm")
    position = jnp.arange(count, dtype=jnp.int32)
    between = (position[None, :] > position[:, None]) & (position[None, :] < own_index)
    factors = jnp.prod(jnp.where(between[:, :, None], decay_table[None, :, :], 1.0), axis=1)
    weights = jnp.where((position < own_index)[:, None], factors, 0.0)
    incoming = jnp.einsum(
        "js,jhws->hws",
        weights,
        lax.all_gather(local_end[None], "tm", axis=0, tiled=True),
        precision=lax.Precision.HIGHEST,
    )
    states = local_states + products[:, None, None, :] * incoming[None]
    rounded_states = states.astype(jnp.bfloat16)
    cycle = with_halo(rounded_states, (("rows", 1), ("cols", 2)), 1)
    mixed = stencil(cycle, output_kernel) + skip_gain * latent_video.astype(jnp.float32)
    return mixed.astype(jnp.bfloat16)


def solution(mesh):
    return jax.shard_map(
        on_device,
        mesh=mesh,
        in_specs=(P("tm", "rows", "cols", None), P(), P(), P("tm", None), P()),
        out_specs=P("tm", "rows", "cols", None),
        check_vma=False,
    )
```

profile of v0, /device:TPU:5, one launch (start us, length us, event | category | flops | bytes accessed | tf_op | source)
XLA Modules:
  0.0 200.5 jit_solution(12926026952751738544)
XLA Ops:
  6.5 0.8 fusion.99
  7.4 3.2 %collective-permute-start = (bf16[6,1,32,128]{3,2,1,0:T(8,128)(2,1)S(1)}, bf16[6,1,32,128]{3,2,1,0:T(8,128)(2,1)S(1)}, u32[]{:S(2)}, u32[]{:S(2)}) collective-permute-start(bf16[6,1,32,128]{3,2,1,0:T(8,128)(2,1)S(1)} %get-tuple-element.97), channel_id=1, source_target_pairs={{0,2},{2,4},{4,6},{1,3},{3,5},{5,7},{8,10},{10,12},{12,14},{9,11},... | collective-permute-start | bytes 147464 | tf_op jit(solution)/shard_map/ppermute | solution.py:12
  10.6 1.4 collective-permute-start.1
  12.0 5.0 %fusion.62 = f32[6,32,32,256]{3,2,1,0:T(8,128)} fusion(bf16[6,32,32,128]{3,2,1,0:T(8,128)(2,1)} %param.7, bf16[3,3,128,256]{3,2,1,0:T(8,128)(2,1)} %param.8), kind=kOutput, calls=%fused_computation.78 | convolution fusion | flops 402653184 | bytes 7929856 | tf_op jit(solution)/shard_map/fhwc,cs->fhws/dot_general | solution.py:27
  17.1 0.4 constant_dynamic-update-slice_fusion.1
  17.7 2.9 %collective-permute-start.3 = (bf16[6,34,1,128]{3,2,1,0:T(2,128)(2,1)S(1)}, bf16[6,34,1,128]{3,2,1,0:T(2,128)(2,1)S(1)}, u32[]{:S(2)}, u32[]{:S(2)}) collective-permute-start(bf16[6,34,1,128]{3,2,1,0:T(2,128)(2,1)S(1)} %get-tuple-element.95), channel_id=1, source_target_pairs={{1,0},{3,2},{5,4},{7,6},{9,8},{11,10},{13,12},{15,14},{17,16},{19,... | collective-permute-start | bytes 156680 | tf_op jit(solution)/shard_map/ppermute | solution.py:15
  20.5 1.4 collective-permute-start.2
  22.0 4.4 %fusion.20 = f32[6,32,32,256]{3,2,1,0:T(8,128)} fusion(bf16[6,32,32,128]{3,2,1,0:T(8,128)(2,1)S(1)} %copy-done, bf16[6,1,32,128]{3,2,1,0:T(8,128)(2,1)S(1)} %collective-permute-done, bf16[3,3,128,256]{3,2,1,0:T(8,128)(2,1)} %param.8), kind=kOutput, calls=%fused_computation.39 | convolution fusion | flops 405897216 | bytes 7979008 | tf_op jit(solution)/shard_map/fhwc,cs->fhws/dot_general | solution.py:27
  26.4 3.6 %fusion.24 = f32[6,32,32,256]{3,2,1,0:T(8,128)} fusion(bf16[6,1,32,128]{3,2,1,0:T(8,128)(2,1)S(1)} %collective-permute-done.1, bf16[6,32,32,128]{3,2,1,0:T(8,128)(2,1)S(1)} %copy-done, bf16[3,3,128,256]{3,2,1,0:T(8,128)(2,1)S(1)} %copy-done.1), kind=kOutput, calls=%fused_computation.43 | convolution fusion | flops 405897216 | bytes 7979008 | tf_op jit(solution)/shard_map/fhwc,cs->fhws/dot_general | solution.py:27
  29.9 3.7 %fusion.29 = f32[6,32,32,256]{3,2,1,0:T(8,128)} fusion(bf16[6,34,32,128]{3,2,1,0:T(8,128)(2,1)S(1)} %constant_dynamic-update-slice_fusion, bf16[6,34,1,128]{3,2,1,0:T(2,128)(2,1)S(1)} %collective-permute-done.3, bf16[3,3,128,256]{3,2,1,0:T(8,128)(2,1)S(1)} %copy-done.1), kind=kOutput, calls=%fused_computation.48 | convolution fusion | flops 405798912 | bytes 8132608 | tf_op jit(solution)/shard_map/fhwc,cs->fhws/dot_general | solution.py:27
  33.6 3.6 %fusion.32 = f32[6,32,32,256]{3,2,1,0:T(8,128)} fusion(bf16[6,34,32,128]{3,2,1,0:T(8,128)(2,1)S(1)} %constant_dynamic-update-slice_fusion, bf16[6,34,1,128]{3,2,1,0:T(2,128)(2,1)S(1)} %collective-permute-done.3, bf16[3,3,128,256]{3,2,1,0:T(8,128)(2,1)S(1)} %copy-done.1), kind=kOutput, calls=%fused_computation.50 | convolution fusion | flops 405798912 | bytes 8132608 | tf_op jit(solution)/shard_map/fhwc,cs->fhws/dot_general | solution.py:27
  37.2 3.7 %fusion.35 = f32[6,32,32,256]{3,2,1,0:T(8,128)} fusion(bf16[6,34,32,128]{3,2,1,0:T(8,128)(2,1)S(1)} %constant_dynamic-update-slice_fusion, bf16[6,34,1,128]{3,2,1,0:T(2,128)(2,1)S(1)} %collective-permute-done.2, bf16[3,3,128,256]{3,2,1,0:T(8,128)(2,1)S(1)} %copy-done.1), kind=kOutput, calls=%fused_computation.52 | convolution fusion | flops 405798912 | bytes 8132608 | tf_op jit(solution)/shard_map/fhwc,cs->fhws/dot_general | solution.py:27
  40.9 3.6 %fusion.38 = f32[6,32,32,256]{3,2,1,0:T(8,128)} fusion(bf16[6,34,32,128]{3,2,1,0:T(8,128)(2,1)S(1)} %constant_dynamic-update-slice_fusion, bf16[6,34,1,128]{3,2,1,0:T(2,128)(2,1)S(1)} %collective-permute-done.2, bf16[3,3,128,256]{3,2,1,0:T(8,128)(2,1)S(1)} %copy-done.1), kind=kOutput, calls=%fused_computation.54 | convolution fusion | flops 405798912 | bytes 8132608 | tf_op jit(solution)/shard_map/fhwc,cs->fhws/dot_general | solution.py:27
  44.5 3.6 %fusion.42 = f32[6,32,32,256]{3,2,1,0:T(8,128)} fusion(bf16[6,34,32,128]{3,2,1,0:T(8,128)(2,1)S(1)} %constant_dynamic-update-slice_fusion, bf16[6,34,1,128]{3,2,1,0:T(2,128)(2,1)S(1)} %collective-permute-done.2, bf16[3,3,128,256]{3,2,1,0:T(8,128)(2,1)S(1)} %copy-done.1), kind=kOutput, calls=%fused_computation.59 | convolution fusion | flops 405798912 | bytes 8132608 | tf_op jit(solution)/shard_map/fhwc,cs->fhws/dot_general | solution.py:27
  48.0 19.6 %add_add_fusion = f32[6,32,32,256]{3,2,1,0:T(8,128)} fusion(f32[6,32,32,256]{3,2,1,0:T(8,128)} %fusion.24, f32[6,32,32,256]{3,2,1,0:T(8,128)} %fusion.42, f32[6,32,32,256]{3,2,1,0:T(8,128)} %fusion.29, f32[6,32,32,256]{3,2,1,0:T(8,128)} %fusion.62, f32[6,32,32,256]{3,2,1,0:T(8,128)} %fusion.35, f32[6,32,32,256]{3,2,1,0:T(8,128)} %fusion.32, ...), kind=kOutput, calls=%fused_computation.6 | convolution fusion | flops 418381824 | bytes 58412032 | tf_op jit(solution)/shard_map/fhwc,cs->fhws/dot_general | solution.py:27
  67.6 23.6 %while.17 = (s32[]{:T(128)}, f32[32,32,256]{2,1,0:T(8,128)}, f32[256]{0:T(256)S(1)}, f32[6,32,32,256]{3,2,1,0:T(8,128)}, f32[6,256]{1,0:T(8,128)S(1)}, /*index=5...) while((s32[]{:T(128)}, f32[32,32,256]{2,1,0:T(8,128)}, f32[256]{0:T(256)S(1)}, ...), condition=%wide.region_1.2_spmd.clone, body=%wide.region_0.1_spmd.clone.sunk | while | flops 786947 | bytes 4203120 | solution.py:48
  67.6 0.7 constant_dynamic-slice_fusion.2
  68.3 2.9 %bitcast_dynamic-update-slice_fusion.2 = (f32[6,32,32,256]{3,2,1,0:T(8,128)}, f32[32,32,256]{2,1,0:T(8,128)}) fusion(f32[6,32,32,256]{3,2,1,0:T(8,128)} %get-tuple-element.158, s32[]{:T(128)} %get-tuple-element.155, f32[6,32,32,256]{3,2,1,0:T(8,128)} %get-tuple-element.170, f32[32,32,256]{2,1,0:T(8,128)} %get-tuple-element.156, pred[]{:T(512)S(6)} %compare.3, ...), kind=kLoop, calls=%fused_computation.clone.1 | loop fusion | flops 786432 | bytes 4195841 | tf_op jit(solution)/shard_map/while/body/jit(dynamic_update_index_in_dim)/dynamic_update_slice | solution.py:48
  71.3 0.7 constant_dynamic-slice_fusion.2
  72.0 3.2 %bitcast_dynamic-update-slice_fusion.2 = (f32[6,32,32,256]{3,2,1,0:T(8,128)}, f32[32,32,256]{2,1,0:T(8,128)}) fusion(f32[6,32,32,256]{3,2,1,0:T(8,128)} %get-tuple-element.158, s32[]{:T(128)} %get-tuple-element.155, f32[6,32,32,256]{3,2,1,0:T(8,128)} %get-tuple-element.170, f32[32,32,256]{2,1,0:T(8,128)} %get-tuple-element.156, pred[]{:T(512)S(6)} %compare.3, ...), kind=kLoop, calls=%fused_computation.clone.1 | loop fusion | flops 786432 | bytes 4195841 | tf_op jit(solution)/shard_map/while/body/jit(dynamic_update_index_in_dim)/dynamic_update_slice | solution.py:48
  75.3 0.7 constant_dynamic-slice_fusion.2
  76.0 3.2 %bitcast_dynamic-update-slice_fusion.2 = (f32[6,32,32,256]{3,2,1,0:T(8,128)}, f32[32,32,256]{2,1,0:T(8,128)}) fusion(f32[6,32,32,256]{3,2,1,0:T(8,128)} %get-tuple-element.158, s32[]{:T(128)} %get-tuple-element.155, f32[6,32,32,256]{3,2,1,0:T(8,128)} %get-tuple-element.170, f32[32,32,256]{2,1,0:T(8,128)} %get-tuple-element.156, pred[]{:T(512)S(6)} %compare.3, ...), kind=kLoop, calls=%fused_computation.clone.1 | loop fusion | flops 786432 | bytes 4195841 | tf_op jit(solution)/shard_map/while/body/jit(dynamic_update_index_in_dim)/dynamic_update_slice | solution.py:48
  79.2 0.7 constant_dynamic-slice_fusion.2
  79.9 3.3 %bitcast_dynamic-update-slice_fusion.2 = (f32[6,32,32,256]{3,2,1,0:T(8,128)}, f32[32,32,256]{2,1,0:T(8,128)}) fusion(f32[6,32,32,256]{3,2,1,0:T(8,128)} %get-tuple-element.158, s32[]{:T(128)} %get-tuple-element.155, f32[6,32,32,256]{3,2,1,0:T(8,128)} %get-tuple-element.170, f32[32,32,256]{2,1,0:T(8,128)} %get-tuple-element.156, pred[]{:T(512)S(6)} %compare.3, ...), kind=kLoop, calls=%fused_computation.clone.1 | loop fusion | flops 786432 | bytes 4195841 | tf_op jit(solution)/shard_map/while/body/jit(dynamic_update_index_in_dim)/dynamic_update_slice | solution.py:48
  83.3 0.7 constant_dynamic-slice_fusion.2
  84.0 3.2 %bitcast_dynamic-update-slice_fusion.2 = (f32[6,32,32,256]{3,2,1,0:T(8,128)}, f32[32,32,256]{2,1,0:T(8,128)}) fusion(f32[6,32,32,256]{3,2,1,0:T(8,128)} %get-tuple-element.158, s32[]{:T(128)} %get-tuple-element.155, f32[6,32,32,256]{3,2,1,0:T(8,128)} %get-tuple-element.170, f32[32,32,256]{2,1,0:T(8,128)} %get-tuple-element.156, pred[]{:T(512)S(6)} %compare.3, ...), kind=kLoop, calls=%fused_computation.clone.1 | loop fusion | flops 786432 | bytes 4195841 | tf_op jit(solution)/shard_map/while/body/jit(dynamic_update_index_in_dim)/dynamic_update_slice | solution.py:48
  87.3 0.7 constant_dynamic-slice_fusion.2
  88.0 3.3 %bitcast_dynamic-update-slice_fusion.2 = (f32[6,32,32,256]{3,2,1,0:T(8,128)}, f32[32,32,256]{2,1,0:T(8,128)}) fusion(f32[6,32,32,256]{3,2,1,0:T(8,128)} %get-tuple-element.158, s32[]{:T(128)} %get-tuple-element.155, f32[6,32,32,256]{3,2,1,0:T(8,128)} %get-tuple-element.170, f32[32,32,256]{2,1,0:T(8,128)} %get-tuple-element.156, pred[]{:T(512)S(6)} %compare.3, ...), kind=kLoop, calls=%fused_computation.clone.1 | loop fusion | flops 786432 | bytes 4195841 | tf_op jit(solution)/shard_map/while/body/jit(dynamic_update_index_in_dim)/dynamic_update_slice | solution.py:48
  91.3 6.0 %all-gather.2 = f32[4,1,256]{2,1,0:T(1,128)S(1)} all-gather(f32[1,1,256]{2,1,0:T(1,128)S(1)} %bitcast.158), channel_id=3, replica_groups=mesh['tm'=4,'rows'=4,'cols'=2] {'tm'}, dimensions={0}, use_global_device_ids=true | all-gather | bytes 5120 | tf_op jit(solution)/shard_map/all_gather | solution.py:51
  97.5 49.3 %all-gather.5.cloned.1.call-done = f32[128,32,256]{2,1,0:T(8,128)} async-done(((f32[32,32,256]{2,1,0:T(8,128)}), f32[128,32,256]{2,1,0:T(8,128)}) %all-gather.5.cloned.1.call-update) | async-done | bytes 4194320 | tf_op jit(solution)/shard_map/all_gather | solution.py:61
  146.9 2.8 %multiply_reduce_fusion = f32[256,32,32]{0,2,1:T(8,128)S(1)} fusion(f32[256,4,32,32]{0,3,2,1:T(8,128)} %bitcast.153, f32[256,4]{0,1:T(4,128)S(1)} %select_bitcast_fusion), kind=kLoop, calls=%fused_computation.7 | loop fusion | flops 1835008 | bytes 5246976 | tf_op jit(solution)/shard_map/js,jhws->hws/dot_general | solution.py:58
  149.7 3.9 %add_convert_fusion = bf16[6,32,32,256]{3,2,1,0:T(8,128)(2,1)S(1)} fusion(f32[6,32,32,256]{3,2,1,0:T(8,128)} %get-tuple-element.45, f32[32,32,256]{2,1,0:T(8,128)S(1)} %bitcast.154, f32[6,256]{1,0:T(8,128)S(1)} %get-tuple-element.46), kind=kLoop, calls=%fused_computation.5 | loop fusion | flops 4718592 | bytes 10491904 | tf_op jit(solution)/shard_map/convert_element_type | solution.py:65
  153.7 3.1 %collective-permute-start.4 = (bf16[6,1,32,256]{3,2,1,0:T(8,128)(2,1)S(1)}, bf16[6,1,32,256]{3,2,1,0:T(8,128)(2,1)S(1)}, u32[]{:S(2)}, u32[]{:S(2)}) collective-permute-start(bf16[6,1,32,256]{3,2,1,0:T(8,128)(2,1)S(1)} %get-tuple-element.93), channel_id=1, source_target_pairs={{0,2},{2,4},{4,6},{1,3},{3,5},{5,7},{8,10},{10,12},{12,14},{9,11},... | collective-permute-start | bytes 294920 | tf_op jit(solution)/shard_map/ppermute | solution.py:12
  156.8 1.5 collective-permute-start.5
  158.3 1.0 fusion.52
  159.3 2.9 %collective-permute-done.5 = bf16[6,1,32,256]{3,2,1,0:T(8,128)(2,1)S(1)} collective-permute-done((bf16[6,1,32,256]{3,2,1,0:T(8,128)(2,1)S(1)}, bf16[6,1,32,256]{3,2,1,0:T(8,128)(2,1)S(1)}, u32[]{:S(2)}, u32[]{:S(2)}) %collective-permute-start.5) | collective-permute-done | bytes 98336 | tf_op jit(solution)/shard_map/ppermute | solution.py:15
  162.1 0.3 pad_maximum_fusion.7
  162.5 1.3 collective-permute-start.6
  163.8 4.0 %collective-permute-start.7 = (bf16[6,34,1,256]{3,2,1,0:T(2,128)(2,1)S(1)}, bf16[6,34,1,256]{3,2,1,0:T(2,128)(2,1)S(1)}, u32[]{:S(2)}, u32[]{:S(2)}) collective-permute-start(bf16[6,34,1,256]{3,2,1,0:T(2,128)(2,1)S(1)} %get-tuple-element.91), channel_id=1, source_target_pairs={{1,0},{3,2},{5,4},{7,6},{9,8},{11,10},{13,12},{15,14},{17,16},{19,... | collective-permute-start | bytes 313352 | tf_op jit(solution)/shard_map/ppermute | solution.py:15
  167.8 2.6 %fusion = f32[6,32,32,128]{3,2,1,0:T(8,128)} fusion(bf16[6,32,32,256]{3,2,1,0:T(8,128)(2,1)S(1)} %add_convert_fusion, bf16[6,1,32,256]{3,2,1,0:T(8,128)(2,1)S(1)} %collective-permute-done.4, bf16[3,3,256,128]{3,2,1,0:T(8,128)(2,1)S(1)} %copy-done.2), kind=kOutput, calls=%fused_computation.10 | convolution fusion | flops 409141248 | bytes 6455296 | tf_op jit(solution)/shard_map/fhwc,cs->fhws/dot_general | solution.py:27
  170.4 2.6 %fusion.4 = f32[6,32,32,128]{3,2,1,0:T(8,128)} fusion(bf16[6,1,32,256]{3,2,1,0:T(8,128)(2,1)S(1)} %collective-permute-done.5, bf16[6,32,32,256]{3,2,1,0:T(8,128)(2,1)S(1)} %add_convert_fusion, bf16[3,3,256,128]{3,2,1,0:T(8,128)(2,1)S(1)} %copy-done.2), kind=kOutput, calls=%fused_computation.14 | convolution fusion | flops 409141248 | bytes 6455296 | tf_op jit(solution)/shard_map/fhwc,cs->fhws/dot_general | solution.py:27
  173.1 2.9 %pad_maximum_fusion = (bf16[6,34,33,256]{3,2,1,0:T(8,128)(2,1)S(1)}, bf16[6,34,33,256]{3,2,1,0:T(8,128)(2,1)S(1)}) fusion(bf16[6,34,1,256]{3,2,1,0:T(2,128)(2,1)S(1)} %collective-permute-done.7, bf16[6,1,32,256]{3,2,1,0:T(8,128)(2,1)S(1)} %collective-permute-done.5, bf16[6,32,32,256]{3,2,1,0:T(8,128)(2,1)S(1)} %add_convert_fusion, ...), kind=kLoop, calls=%fused_computation.9 | loop fusion | flops 27574272 | bytes 10444800 | tf_op jit(solution)/shard_map/concatenate | solution.py:16
  176.0 1.0 fusion.10
  177.0 1.0 fusion.14
  177.9 2.7 %fusion.12 = f32[6,32,32,128]{3,2,1,0:T(8,128)} fusion(bf16[6,34,33,256]{3,2,1,0:T(8,128)(2,1)S(1)} %get-tuple-element.89, bf16[3,3,256,128]{3,2,1,0:T(8,128)(2,1)S(1)} %copy-done.2), kind=kOutput, calls=%fused_computation.22 | convolution fusion | flops 402653184 | bytes 6356992 | tf_op jit(solution)/shard_map/fhwc,cs->fhws/dot_general | solution.py:27
  180.6 2.7 %fusion.16 = f32[6,32,32,128]{3,2,1,0:T(8,128)} fusion(bf16[6,34,33,256]{3,2,1,0:T(8,128)(2,1)S(1)} %get-tuple-element.89, bf16[3,3,256,128]{3,2,1,0:T(8,128)(2,1)S(1)} %copy-done.2), kind=kOutput, calls=%fused_computation.26 | convolution fusion | flops 402653184 | bytes 6356992 | tf_op jit(solution)/shard_map/fhwc,cs->fhws/dot_general | solution.py:27
  183.3 2.6 %fusion.18 = f32[6,32,32,128]{3,2,1,0:T(8,128)} fusion(bf16[6,34,33,256]{3,2,1,0:T(8,128)(2,1)S(1)} %get-tuple-element.90, bf16[3,3,256,128]{3,2,1,0:T(8,128)(2,1)S(1)} %copy-done.2), kind=kOutput, calls=%fused_computation.28 | convolution fusion | flops 402653184 | bytes 6356992 | tf_op jit(solution)/shard_map/fhwc,cs->fhws/dot_general | solution.py:27
  186.0 7.7 %add_convert_fusion.1 = bf16[6,32,32,128]{3,2,1,0:T(8,128)(2,1)} fusion(bf16[6,32,32,128]{3,2,1,0:T(8,128)(2,1)S(1)} %copy-done, f32[6,32,32,128]{3,2,1,0:T(8,128)} %fusion.4, f32[6,32,32,128]{3,2,1,0:T(8,128)S(1)} %fusion.10, f32[6,32,32,128]{3,2,1,0:T(8,128)} %fusion.12, f32[6,32,32,128]{3,2,1,0:T(8,128)S(1)} %fusion.52, ...), kind=kOutput, calls=%fused_computation.30 | convolution fusion | flops 412090368 | bytes 31523328 | tf_op jit(solution)/shard_map/fhwc,cs->fhws/dot_general | solution.py:27
  (42 shorter events, 0.7 us)
Async XLA Ops:
  6.5 140.3 %all-gather.5.cloned.1.call-start = ((), (), s32[]{:S(2)}) async-start(), calls=%async_computation | async-start | bytes 5242880 | tf_op jit(solution)/shard_map/all_gather | solution.py:61
  7.4 9.7 %collective-permute-start = (bf16[6,1,32,128]{3,2,1,0:T(8,128)(2,1)S(1)}, bf16[6,1,32,128]{3,2,1,0:T(8,128)(2,1)S(1)}, u32[]{:S(2)}, u32[]{:S(2)}) collective-permute-start(bf16[6,1,32,128]{3,2,1,0:T(8,128)(2,1)S(1)} %get-tuple-element.97), channel_id=1, source_target_pairs={{0,2},{2,4},{4,6},{1,3},{3,5},{5,7},{8,10},{10,12},{12,14},{9,11},... | collective-permute-start | bytes 147464 | tf_op jit(solution)/shard_map/ppermute | solution.py:12
  10.6 6.5 %copy-start = (bf16[6,32,32,128]{3,2,1,0:T(8,128)(2,1)S(1)}, bf16[6,32,32,128]{3,2,1,0:T(8,128)(2,1)}, u32[]{:S(2)}) copy-start(bf16[6,32,32,128]{3,2,1,0:T(8,128)(2,1)} %param.7) | copy-start | bytes 4718596
  10.6 6.9 %collective-permute-start.1 = (bf16[6,1,32,128]{3,2,1,0:T(8,128)(2,1)S(1)}, bf16[6,1,32,128]{3,2,1,0:T(8,128)(2,1)S(1)}, u32[]{:S(2)}, u32[]{:S(2)}) collective-permute-start(bf16[6,1,32,128]{3,2,1,0:T(8,128)(2,1)S(1)} %get-tuple-element.98), channel_id=1, source_target_pairs={{2,0},{4,2},{6,4},{3,1},{5,3},{7,5},{10,8},{12,10},{14,12},{11,9},... | collective-permute-start | bytes 147464 | tf_op jit(solution)/shard_map/ppermute | solution.py:15
  17.7 12.3 %collective-permute-start.3 = (bf16[6,34,1,128]{3,2,1,0:T(2,128)(2,1)S(1)}, bf16[6,34,1,128]{3,2,1,0:T(2,128)(2,1)S(1)}, u32[]{:S(2)}, u32[]{:S(2)}) collective-permute-start(bf16[6,34,1,128]{3,2,1,0:T(2,128)(2,1)S(1)} %get-tuple-element.95), channel_id=1, source_target_pairs={{1,0},{3,2},{5,4},{7,6},{9,8},{11,10},{13,12},{15,14},{17,16},{19,... | collective-permute-start | bytes 156680 | tf_op jit(solution)/shard_map/ppermute | solution.py:15
  20.5 5.8 %copy-start.1 = (bf16[3,3,128,256]{3,2,1,0:T(8,128)(2,1)S(1)}, bf16[3,3,128,256]{3,2,1,0:T(8,128)(2,1)}, u32[]{:S(2)}) copy-start(bf16[3,3,128,256]{3,2,1,0:T(8,128)(2,1)} %param.8) | copy-start | bytes 1769476
  20.5 16.7 %collective-permute-start.2 = (bf16[6,34,1,128]{3,2,1,0:T(2,128)(2,1)S(1)}, bf16[6,34,1,128]{3,2,1,0:T(2,128)(2,1)S(1)}, u32[]{:S(2)}, u32[]{:S(2)}) collective-permute-start(bf16[6,34,1,128]{3,2,1,0:T(2,128)(2,1)S(1)} %get-tuple-element.96), channel_id=1, source_target_pairs={{0,1},{2,3},{4,5},{6,7},{8,9},{10,11},{12,13},{14,15},{16,17},{18,... | collective-permute-start | bytes 156680 | tf_op jit(solution)/shard_map/ppermute | solution.py:12
  149.7 8.6 %copy-start.2 = (bf16[3,3,256,128]{3,2,1,0:T(8,128)(2,1)S(1)}, bf16[3,3,256,128]{3,2,1,0:T(8,128)(2,1)}, u32[]{:S(2)}) copy-start(bf16[3,3,256,128]{3,2,1,0:T(8,128)(2,1)} %param.9) | copy-start | bytes 1769476
  153.7 5.6 %collective-permute-start.4 = (bf16[6,1,32,256]{3,2,1,0:T(8,128)(2,1)S(1)}, bf16[6,1,32,256]{3,2,1,0:T(8,128)(2,1)S(1)}, u32[]{:S(2)}, u32[]{:S(2)}) collective-permute-start(bf16[6,1,32,256]{3,2,1,0:T(8,128)(2,1)S(1)} %get-tuple-element.93), channel_id=1, source_target_pairs={{0,2},{2,4},{4,6},{1,3},{3,5},{5,7},{8,10},{10,12},{12,14},{9,11},... | collective-permute-start | bytes 294920 | tf_op jit(solution)/shard_map/ppermute | solution.py:12
  156.8 5.4 %collective-permute-start.5 = (bf16[6,1,32,256]{3,2,1,0:T(8,128)(2,1)S(1)}, bf16[6,1,32,256]{3,2,1,0:T(8,128)(2,1)S(1)}, u32[]{:S(2)}, u32[]{:S(2)}) collective-permute-start(bf16[6,1,32,256]{3,2,1,0:T(8,128)(2,1)S(1)} %get-tuple-element.94), channel_id=1, source_target_pairs={{2,0},{4,2},{6,4},{3,1},{5,3},{7,5},{10,8},{12,10},{14,12},{11,9},... | collective-permute-start | bytes 294920 | tf_op jit(solution)/shard_map/ppermute | solution.py:15
  162.5 10.6 %collective-permute-start.6 = (bf16[6,34,1,256]{3,2,1,0:T(2,128)(2,1)S(1)}, bf16[6,34,1,256]{3,2,1,0:T(2,128)(2,1)S(1)}, u32[]{:S(2)}, u32[]{:S(2)}) collective-permute-start(bf16[6,34,1,256]{3,2,1,0:T(2,128)(2,1)S(1)} %get-tuple-element.92), channel_id=1, source_target_pairs={{0,1},{2,3},{4,5},{6,7},{8,9},{10,11},{12,13},{14,15},{16,17},{18,... | collective-permute-start | bytes 313352 | tf_op jit(solution)/shard_map/ppermute | solution.py:12
  163.8 9.3 %collective-permute-start.7 = (bf16[6,34,1,256]{3,2,1,0:T(2,128)(2,1)S(1)}, bf16[6,34,1,256]{3,2,1,0:T(2,128)(2,1)S(1)}, u32[]{:S(2)}, u32[]{:S(2)}) collective-permute-start(bf16[6,34,1,256]{3,2,1,0:T(2,128)(2,1)S(1)} %get-tuple-element.91), channel_id=1, source_target_pairs={{1,0},{3,2},{5,4},{7,6},{9,8},{11,10},{13,12},{15,14},{17,16},{19,... | collective-permute-start | bytes 313352 | tf_op jit(solution)/shard_map/ppermute | solution.py:15
  183.3 2.6 %copy-start.3 = (f32[128]{0:T(128)S(1)}, f32[128]{0:T(128)}, u32[]{:S(2)}) copy-start(f32[128]{0:T(128)} %param.11) | copy-start | bytes 1540
Sparse Core Ops, SparseCore 0:
  91.4 55.4 all-gather.4
where the time goes:
time: 202 us; the launch traced here: 201 us
  matrix products  74.5 us (37%)
  waiting for transfers between devices  52.3 us (26%)
  other arithmetic  29.4 us (15%)
  starting transfers between devices  18.8 us (9%)
  between operations  13.6 us (7%)
  blocking collectives  6.03 us (3%)
  local copies, waits for them, and re-layouts  5.83 us (3%)
    dot_general x18, matrix products, stencil(): jnp.einsum('fhwc,cs->fhws', window, kernel[row_off, col_off], preferred_e...  74.5 us
    all_gather x1, waiting for transfers between devices, on_device(): lax.all_gather(local_end[None], 'tm', axis=0, tiled=True)  49.3 us
    dynamic_update_slice x6, other arithmetic, on_device(): finals, history = lax.scan(advance, start, (drive, decay_rate))  19.1 us
    ppermute x4, starting transfers between devices, with_halo(): lax.ppermute(lax.slice_in_dim(block, 0, width, axis=dim), axis, backward)  9.8 us
    ppermute x4, starting transfers between devices, with_halo(): lax.ppermute(lax.slice_in_dim(block, block.shape[dim] - width, None, axis...  9.02 us
    all_gather x1, blocking collectives, on_device(): decay_table = lax.all_gather(block_decay[None, :], 'tm', axis=0, tiled=True)  6.03 us
    dynamic_slice x6, local copies, waits for them, and re-layouts, on_device(): finals, history = lax.scan(advance, start, (drive, decay_rate))  4.23 us
  transfers between devices with their start and end apart: 9, of which 2 were waited for; matrix products, arithmetic and copies ran while one was open for 13% of the time, Pallas kernels for 0%

commit v1 on v0

v1 whole, which is shorter than its diff:
```python
import functools

import jax
import jax.numpy as jnp
from jax import lax
from jax.experimental import pallas as pl
from jax.experimental.pallas import tpu as pltpu
from jax.sharding import PartitionSpec as P

MESH = pl.DeviceIdType.MESH
STEP = 2
LAG = 3


def layer_kernel(
    blocks, tiles, x_ref, w1_ref, w2_ref, decay_ref, skip_ref, out_ref,
    xp, xs, local, st, w1, w2, decay, skip, carry_in, carry_out, result,
    load_sem, w2_sem, side_send, side_recv, z_send, z_recv,
    carry_send, carry_recv, out_sem, out_send, out_recv,
):
    frames, tile_h, tile_w, cin = x_ref.shape
    state = w1.shape[1]
    half = tile_h // 2
    width = 2 * tile_w
    chunks = (half + 2) // STEP
    flat = STEP * width
    t = lax.axis_index("tm")
    z = lax.axis_index("rows")
    c = lax.axis_index("cols")
    o = 1 - c
    has_up = z > 0
    has_down = z < tiles - 1
    has_next = t < blocks - 1
    own_cols = pl.ds(pl.multiple_of(c * tile_w, tile_w), tile_w)
    other_cols = pl.ds(pl.multiple_of(o * tile_w, tile_w), tile_w)

    loads = [
        pltpu.make_async_copy(
            x_ref.at[:, pl.ds((half - 2) * c, half + 2)],
            xp.at[:, pl.ds(2 * o, half + 2), own_cols],
            load_sem.at[0],
        ),
        pltpu.make_async_copy(w1_ref, w1, load_sem.at[1]),
        pltpu.make_async_copy(decay_ref, decay, load_sem.at[2]),
        pltpu.make_async_copy(skip_ref, skip, load_sem.at[3]),
    ]
    w2_loads = [
        pltpu.make_async_copy(
            w2_ref.at[a, b],
            w2.at[pl.ds(a * state, state), pl.ds(b * cin, cin)],
            w2_sem.at[3 * a + b],
        )
        for a in range(3)
        for b in range(3)
    ]
    for copy in loads + w2_loads:
        copy.start()

    barrier = pltpu.get_barrier_semaphore()
    up_side = jnp.logical_and(c == 0, has_up)
    down_side = jnp.logical_and(c == 1, has_down)
    pl.semaphore_signal(barrier, inc=1, device_id=(t, z, o), device_id_type=MESH)

    @pl.when(up_side)
    def _():
        for core in range(2):
            pl.semaphore_signal(barrier, inc=1, device_id=(t, z - 1, core), device_id_type=MESH)

    @pl.when(down_side)
    def _():
        for core in range(2):
            pl.semaphore_signal(barrier, inc=1, device_id=(t, z + 1, core), device_id_type=MESH)

    @pl.when(t > 0)
    def _():
        pl.semaphore_signal(barrier, inc=1, device_id=(t - 1, z, c), device_id_type=MESH)

    @pl.when(jnp.logical_and(c == 0, z == 0))
    def _():
        xp[:, 0:2] = jnp.zeros((frames, 2, width, cin), xp.dtype)

    @pl.when(jnp.logical_and(c == 1, z == tiles - 1))
    def _():
        xp[:, half + 2 : half + 4] = jnp.zeros((frames, 2, width, cin), xp.dtype)

    @pl.when(t == 0)
    def _():
        carry_in[...] = jnp.zeros_like(carry_in)

    expected = (
        1 + has_up.astype(jnp.int32) + has_down.astype(jnp.int32) + has_next.astype(jnp.int32)
    )
    pl.semaphore_wait(barrier, expected)

    side = pltpu.make_async_remote_copy(
        src_ref=x_ref.at[:, pl.ds((half - 2) * o, half + 2)],
        dst_ref=xp.at[:, pl.ds(2 * c, half + 2), own_cols],
        send_sem=side_send,
        recv_sem=side_recv,
        device_id=(t, z, o),
        device_id_type=MESH,
    )
    side.start()

    def to_down():
        return pltpu.make_async_remote_copy(
            src_ref=x_ref.at[:, pl.ds(tile_h - 2, 2)],
            dst_ref=xp.at[:, pl.ds(0, 2), own_cols],
            send_sem=z_send.at[0],
            recv_sem=z_recv.at[c],
            device_id=(t, z + 1, 0),
            device_id_type=MESH,
        )

    def to_up():
        return pltpu.make_async_remote_copy(
            src_ref=x_ref.at[:, pl.ds(0, 2)],
            dst_ref=xp.at[:, pl.ds(half + 2, 2), own_cols],
            send_sem=z_send.at[1],
            recv_sem=z_recv.at[c],
            device_id=(t, z - 1, 1),
            device_id_type=MESH,
        )

    @pl.when(has_down)
    def _():
        to_down().start()

    @pl.when(has_up)
    def _():
        to_up().start()

    for copy in loads:
        copy.wait()
    pltpu.make_async_remote_copy(
        src_ref=x_ref.at[:, pl.ds((half - 2) * o, half + 2)],
        dst_ref=xp.at[:, pl.ds(2 * o, half + 2), other_cols],
        send_sem=side_send,
        recv_sem=side_recv,
        device_id=(t, z, o),
        device_id_type=MESH,
    ).wait_recv()

    def columns(rows):
        return lax.rem(lax.broadcasted_iota(jnp.int32, (rows, 128), 0), width)

    def spread(row):
        view = xp[:, pl.ds(row, STEP)].reshape(frames * flat, cin)
        wide = view.astype(jnp.float32)
        at = columns(frames * flat)
        left = jnp.where(at == 0, 0.0, pltpu.roll(wide, 1, 0))
        right = jnp.where(at == width - 1, 0.0, pltpu.roll(wide, frames * flat - 1, 0))
        shape = (frames, STEP, width, cin)
        xs[:, pl.ds(row, STEP), :, 0:cin] = left.astype(xs.dtype).reshape(shape)
        xs[:, pl.ds(row, STEP), :, cin : 2 * cin] = view.reshape(shape)
        xs[:, pl.ds(row, STEP), :, 2 * cin : 3 * cin] = right.astype(xs.dtype).reshape(shape)

    def drive_chunk(k):
        @pl.when(k == 0)
        def _():
            spread((half + 2) * o)

        @pl.when(k == chunks - 1)
        def _():
            @pl.when(jnp.logical_or(up_side, down_side))
            def _():
                for core in range(2):
                    rows = pl.ds((half + 2) * c, 2)
                    pltpu.make_async_remote_copy(
                        src_ref=x_ref.at[:, pl.ds(0, 2)],
                        dst_ref=xp.at[:, rows, pl.ds(core * tile_w, tile_w)],
                        send_sem=z_send.at[0],
                        recv_sem=z_recv.at[core],
                        device_id=(t, z, o),
                        device_id_type=MESH,
                    ).wait_recv()

        spread(jnp.where(c == 0, half - STEP * k, STEP * k + 2))
        row = jnp.where(c == 0, half - STEP * k, STEP * k)
        lhs = jnp.concatenate(
            [xs[:, pl.ds(row + a, STEP)].reshape(frames * flat, 3 * cin) for a in range(3)],
            axis=1,
        )
        drive = jnp.dot(lhs, w1[...], preferred_element_type=jnp.float32)
        running = drive[0:flat]
        local[k, 0] = running
        for f in range(1, frames):
            running = decay[f : f + 1, :] * running + drive[f * flat : (f + 1) * flat]
            local[k, f] = running

    def carry_copy(k):
        return pltpu.make_async_remote_copy(
            src_ref=carry_out.at[k],
            dst_ref=carry_in.at[k],
            send_sem=carry_send.at[k],
            recv_sem=carry_recv.at[k],
            device_id=(t + 1, z, c),
            device_id_type=MESH,
        )

    def out_copies(k):
        row = jnp.where(c == 0, half - STEP * k, STEP * k - 2)
        to = out_ref.at[:, pl.ds(half * c + row, STEP)]
        own = pltpu.make_async_copy(
            result.at[:, pl.ds(row, STEP), own_cols], to, out_sem.at[k]
        )
        far = pltpu.make_async_remote_copy(
            src_ref=result.at[:, pl.ds(row, STEP), other_cols],
            dst_ref=to,
            send_sem=out_send.at[k],
            recv_sem=out_recv.at[k],
            device_id=(t, z, o),
            device_id_type=MESH,
        )
        return own, far

    def mix_chunk(k):
        row = jnp.where(c == 0, half - STEP * k, STEP * k - 2)
        lhs = jnp.concatenate(
            [st[:, pl.ds(row + a, STEP)].reshape(frames * flat, state) for a in range(3)],
            axis=1,
        )
        taps = jnp.dot(lhs, w2[...], preferred_element_type=jnp.float32)
        at = columns(frames * flat)
        left = jnp.where(at == 0, 0.0, pltpu.roll(taps[:, 0:cin], 1, 0))
        right = jnp.where(
            at == width - 1, 0.0, pltpu.roll(taps[:, 2 * cin : 3 * cin], frames * flat - 1, 0)
        )
        latent = xp[:, pl.ds(row + 2, STEP)].reshape(frames * flat, cin).astype(jnp.float32)
        mixed = left + taps[:, cin : 2 * cin] + right + skip[...] * latent
        result[:, pl.ds(row, STEP)] = mixed.astype(result.dtype).reshape(
            frames, STEP, width, cin
        )
        for copy in out_copies(k):
            copy.start()

    def forward_chunk(k):
        @pl.when(t > 0)
        def _():
            carry_copy(k).wait_recv()

        @pl.when(has_next)
        def _():
            factor = decay[0:1, :]
            for f in range(1, frames):
                factor = factor * decay[f : f + 1, :]
            ahead = factor * carry_in[k].astype(jnp.float32) + local[k, frames - 1]
            carry_out[k] = ahead.astype(carry_out.dtype)
            carry_copy(k).start()

    def finish_chunk(k):
        row = jnp.where(c == 0, half - STEP * k, STEP * k)
        incoming = carry_in[k].astype(jnp.float32)
        product = decay[0:1, :]
        for f in range(frames):
            if f:
                product = product * decay[f : f + 1, :]
            now = (local[k, f] + product * incoming).astype(st.dtype)
            st[f, pl.ds(row, STEP)] = now.reshape(STEP, width, state)

        @pl.when(k == chunks - 1)
        def _():
            @pl.when(jnp.logical_and(c == 0, z == 0))
            def _():
                st[:, 0:1] = jnp.zeros((frames, 1, width, state), st.dtype)

            @pl.when(jnp.logical_and(c == 1, z == tiles - 1))
            def _():
                st[:, half + 1 : half + 2] = jnp.zeros((frames, 1, width, state), st.dtype)

        @pl.when(k > 0)
        def _():
            mix_chunk(k)

    lag = jnp.minimum(LAG * t, chunks)
    for copy in w2_loads:
        copy.wait()

    def turn(j, carried):
        @pl.when(j < chunks)
        def _():
            drive_chunk(j)

        @pl.when(jnp.logical_and(j >= lag, j - lag < chunks))
        def _():
            forward_chunk(j - lag)

        @pl.when(j >= chunks)
        def _():
            finish_chunk(j - chunks)

        return carried

    lax.fori_loop(0, 2 * chunks, turn, 0)

    side.wait_send()

    @pl.when(has_down)
    def _():
        to_down().wait_send()

    @pl.when(has_up)
    def _():
        to_up().wait_send()

    def finish(k, carried):
        @pl.when(has_next)
        def _():
            carry_copy(k).wait_send()

        @pl.when(k > 0)
        def _():
            own, far = out_copies(k)
            own.wait()
            far.wait_send()
            row = jnp.where(o == 0, half - STEP * k, STEP * k - 2)
            pltpu.make_async_remote_copy(
                src_ref=result.at[:, pl.ds(0, STEP), own_cols],
                dst_ref=out_ref.at[:, pl.ds(half * o + row, STEP)],
                send_sem=out_send.at[k],
                recv_sem=out_recv.at[k],
                device_id=(t, z, o),
                device_id_type=MESH,
            ).wait_recv()

        return carried

    lax.fori_loop(0, chunks, finish, 0)


def on_device(latent_video, input_kernel, output_kernel, decay_rate, skip_gain):
    frames, tile_h, tile_w, cin = latent_video.shape
    state = input_kernel.shape[3]
    blocks = lax.axis_size("tm")
    tiles = lax.axis_size("rows")
    half = tile_h // 2
    width = 2 * tile_w
    chunks = (half + 2) // STEP
    flat = STEP * width
    dma = pltpu.SemaphoreType.DMA
    bf16, f32 = jnp.bfloat16, jnp.float32
    pixels = frames * tile_h * tile_w
    return pl.pallas_call(
        functools.partial(layer_kernel, blocks, tiles),
        out_shape=jax.ShapeDtypeStruct(latent_video.shape, bf16),
        in_specs=[pl.BlockSpec(memory_space=pl.ANY)] * 5,
        out_specs=pl.BlockSpec(memory_space=pl.ANY),
        scratch_shapes=[
            pltpu.VMEM((frames, half + 4, width, cin), bf16),
            pltpu.VMEM((frames, half + 4, width, 3 * cin), bf16),
            pltpu.VMEM((chunks, frames, flat, state), f32),
            pltpu.VMEM((frames, half + 2, width, state), bf16),
            pltpu.VMEM((9 * cin, state), bf16),
            pltpu.VMEM((3 * state, 3 * cin), bf16),
            pltpu.VMEM((frames, state), f32),
            pltpu.VMEM((1, cin), f32),
            pltpu.VMEM((chunks, flat, state), bf16),
            pltpu.VMEM((chunks, flat, state), bf16),
            pltpu.VMEM((frames, half, width, cin), bf16),
            dma((4,)),
            dma((9,)),
            dma,
            dma,
            dma((2,)),
            dma((2,)),
            dma((chunks,)),
            dma((chunks,)),
            dma((chunks,)),
            dma((chunks,)),
            dma((chunks,)),
        ],
        compiler_params=pltpu.CompilerParams(
            collective_id=0, has_side_effects=True, vmem_limit_bytes=64 * 1024 * 1024
        ),
        cost_estimate=pl.CostEstimate(
            flops=4 * pixels * 9 * cin * state, bytes_accessed=8 * pixels * cin, transcendentals=0
        ),
    )(
        latent_video,
        input_kernel.reshape(9 * cin, state),
        output_kernel,
        decay_rate,
        skip_gain.reshape(1, cin),
    )


def solution(mesh):
    return jax.shard_map(
        on_device,
        mesh=mesh,
        in_specs=(P("tm", "rows", "cols", None), P(), P(), P("tm", None), P()),
        out_specs=P("tm", "rows", "cols", None),
        check_vma=False,
    )
```

time: 202 us -> 32.6 us (0.16)
  the two profiles are of different devices: /device:TPU:5 before, /device:TPU:7 now
where the time goes in v1:
time: 32.6 us; the launch traced here: 32.5 us
  Pallas kernels  29.6 us (91%)
  local copies, waits for them, and re-layouts  2.84 us (9%)
    pallas_call x1, Pallas kernels, on_device(): pl.pallas_call(functools.partial(layer_kernel, blocks, tiles), out_shape=...  29.6 us
    unnamed x1, local copies, waits for them, and re-layouts  2.84 us

profile of v1, /device:TPU:7, one launch (start us, length us, event | category | flops | bytes accessed | tf_op | source)
XLA Modules:
  0.0 32.5 jit_solution(1752231493706492886)
XLA Ops:
  0.0 29.6 %shard_map.55 = bf16[6,32,32,128]{3,2,1,0:T(8,128)(2,1)} custom-call(bf16[6,32,32,128]{3,2,1,0:T(8,128)(2,1)} %x_ref.1, bf16[1152,256]{1,0:T(8,128)(2,1)} %bitcast.2, bf16[3,3,256,128]{3,2,1,0:T(8,128)(2,1)} %w2_ref.1, f32[6,256]{1,0:T(8,128)} %decay_ref.1, f32[1,128]{1,0:T(1,128)} %bitcast.3), custom_call_target="tpu_custom_call" | custom-call | flops 7247757312 | bytes 6291456 | tf_op jit(solution)/shard_map/pallas_call | solution.py:343
  29.7 2.8 %copy.7 = bf16[6,32,32,128]{3,2,1,0:T(8,128)(2,1)} copy(bf16[6,32,32,128]{3,2,1,0:T(8,128)(2,1)} %shard_map.55) | data formatting | bytes 3145728

commit v2 on v1

--- a/solution.py
+++ b/solution.py
@@ -14,9 +14,9 @@
 
 def layer_kernel(
     blocks, tiles, x_ref, w1_ref, w2_ref, decay_ref, skip_ref, out_ref,
-    xp, xs, local, st, w1, w2, decay, skip, carry_in, carry_out, result,
+    xp, xs, local, st, w1, w2, decay, skip, carry_in, pair_in, pair_decay, own_decay, carry_out, result,
     load_sem, w2_sem, side_send, side_recv, z_send, z_recv,
-    carry_send, carry_recv, out_sem, out_send, out_recv,
+    decay_send, decay_recv, carry_send, far_send, carry_recv, pair_recv, out_sem, out_send, out_recv,
 ):
     frames, tile_h, tile_w, cin = x_ref.shape
     state = w1.shape[1]
@@ -30,7 +30,11 @@
     o = 1 - c
     has_up = z > 0
     has_down = z < tiles - 1
+    odd = lax.rem(t, 2) == 1
+    even = lax.rem(t, 2) == 0
     has_next = t < blocks - 1
+    has_far = jnp.logical_and(odd, t < blocks - 2)
+    has_carry = t > 1
     own_cols = pl.ds(pl.multiple_of(c * tile_w, tile_w), tile_w)
     other_cols = pl.ds(pl.multiple_of(o * tile_w, tile_w), tile_w)
 
@@ -75,6 +79,10 @@
     def _():
         pl.semaphore_signal(barrier, inc=1, device_id=(t - 1, z, c), device_id_type=MESH)
 
+    @pl.when(jnp.logical_and(odd, has_carry))
+    def _():
+        pl.semaphore_signal(barrier, inc=1, device_id=(t - 2, z, c), device_id_type=MESH)
+
     @pl.when(jnp.logical_and(c == 0, z == 0))
     def _():
         xp[:, 0:2] = jnp.zeros((frames, 2, width, cin), xp.dtype)
@@ -83,12 +91,21 @@
     def _():
         xp[:, half + 2 : half + 4] = jnp.zeros((frames, 2, width, cin), xp.dtype)
 
-    @pl.when(t == 0)
+    @pl.when(t < 2)
     def _():
         carry_in[...] = jnp.zeros_like(carry_in)
 
+    @pl.when(even)
+    def _():
+        pair_in[...] = jnp.zeros_like(pair_in)
+        pair_decay[...] = jnp.ones_like(pair_decay)
+
     expected = (
-        1 + has_up.astype(jnp.int32) + has_down.astype(jnp.int32) + has_next.astype(jnp.int32)
+        1
+        + has_up.astype(jnp.int32)
+        + has_down.astype(jnp.int32)
+        + has_next.astype(jnp.int32)
+        + has_far.astype(jnp.int32)
     )
     pl.semaphore_wait(barrier, expected)
 
@@ -132,6 +149,28 @@
 
     for copy in loads:
         copy.wait()
+
+    block_decay = decay[0:1, :]
+    for f in range(1, frames):
+        block_decay = block_decay * decay[f : f + 1, :]
+    own_decay[...] = jnp.broadcast_to(block_decay, own_decay.shape)
+
+    def decay_copy():
+        return pltpu.make_async_remote_copy(
+            src_ref=own_decay,
+            dst_ref=pair_decay,
+            send_sem=decay_send,
+            recv_sem=decay_recv,
+            device_id=(t + 1, z, c),
+            device_id_type=MESH,
+        )
+
+    sends_pair = jnp.logical_and(even, has_next)
+
+    @pl.when(sends_pair)
+    def _():
+        decay_copy().start()
+
     pltpu.make_async_remote_copy(
         src_ref=x_ref.at[:, pl.ds((half - 2) * o, half + 2)],
         dst_ref=xp.at[:, pl.ds(2 * o, half + 2), other_cols],
@@ -188,15 +227,24 @@
             running = decay[f : f + 1, :] * running + drive[f * flat : (f + 1) * flat]
             local[k, f] = running
 
-    def carry_copy(k):
+    def tm_copy(k, landing, send, recv, hop):
         return pltpu.make_async_remote_copy(
             src_ref=carry_out.at[k],
-            dst_ref=carry_in.at[k],
-            send_sem=carry_send.at[k],
-            recv_sem=carry_recv.at[k],
-            device_id=(t + 1, z, c),
+            dst_ref=landing.at[k],
+            send_sem=send.at[k],
+            recv_sem=recv.at[k],
+            device_id=(t + hop, z, c),
             device_id_type=MESH,
         )
+
+    def pair_copy(k):
+        return tm_copy(k, pair_in, carry_send, pair_recv, 1)
+
+    def next_copy(k):
+        return tm_copy(k, carry_in, carry_send, carry_recv, 1)
+
+    def far_copy(k):
+        return tm_copy(k, carry_in, far_send, carry_recv, 2)
 
     def out_copies(k):
         row = jnp.where(c == 0, half - STEP * k, STEP * k - 2)
@@ -234,23 +282,37 @@
         for copy in out_copies(k):
             copy.start()
 
+    def incoming_of(k):
+        return pair_in[k].astype(jnp.float32) + pair_decay[0:1, :] * carry_in[k].astype(jnp.float32)
+
+    def pair_chunk(k):
+        carry_out[k] = local[k, frames - 1].astype(carry_out.dtype)
+        pair_copy(k).start()
+
     def forward_chunk(k):
-        @pl.when(t > 0)
-        def _():
-            carry_copy(k).wait_recv()
+        @pl.when(k == 0)
+        def _():
+            decay_copy().wait_recv()
+
+        pair_copy(k).wait_recv()
+
+        @pl.when(has_carry)
+        def _():
+            next_copy(k).wait_recv()
 
         @pl.when(has_next)
         def _():
-            factor = decay[0:1, :]
-            for f in range(1, frames):
-                factor = factor * decay[f : f + 1, :]
-            ahead = factor * carry_in[k].astype(jnp.float32) + local[k, frames - 1]
+            ahead = own_decay[0:1, :] * incoming_of(k) + local[k, frames - 1]
             carry_out[k] = ahead.astype(carry_out.dtype)
-            carry_copy(k).start()
+            next_copy(k).start()
+
+            @pl.when(has_far)
+            def _():
+                far_copy(k).start()
 
     def finish_chunk(k):
         row = jnp.where(c == 0, half - STEP * k, STEP * k)
-        incoming = carry_in[k].astype(jnp.float32)
+        incoming = incoming_of(k)
         product = decay[0:1, :]
         for f in range(frames):
             if f:
@@ -272,7 +334,6 @@
         def _():
             mix_chunk(k)
 
-    lag = jnp.minimum(LAG * t, chunks)
     for copy in w2_loads:
         copy.wait()
 
@@ -281,12 +342,27 @@
         def _():
             drive_chunk(j)
 
-        @pl.when(jnp.logical_and(j >= lag, j - lag < chunks))
-        def _():
-            forward_chunk(j - lag)
+            @pl.when(sends_pair)
+            def _():
+                pair_chunk(j)
+
+        since = j - LAG
+        paced = (2 * since + 1) // 3
+
+        @pl.when((t == 1) & (since >= 0) & (lax.rem(since + 3, 3) != 1) & (paced < chunks))
+        def _():
+            forward_chunk(paced)
 
         @pl.when(j >= chunks)
         def _():
+            @pl.when(odd & has_carry)
+            def _():
+                forward_chunk(j - chunks)
+
+            @pl.when(even & has_carry)
+            def _():
+                next_copy(j - chunks).wait_recv()
+
             finish_chunk(j - chunks)
 
         return carried
@@ -294,6 +370,10 @@
     lax.fori_loop(0, 2 * chunks, turn, 0)
 
     side.wait_send()
+
+    @pl.when(sends_pair)
+    def _():
+        decay_copy().wait_send()
 
     @pl.when(has_down)
     def _():
@@ -306,7 +386,11 @@
     def finish(k, carried):
         @pl.when(has_next)
         def _():
-            carry_copy(k).wait_send()
+            next_copy(k).wait_send()
+
+        @pl.when(has_far)
+        def _():
+            far_copy(k).wait_send()
 
         @pl.when(k > 0)
         def _():
@@ -342,9 +426,9 @@
     pixels = frames * tile_h * tile_w
     return pl.pallas_call(
         functools.partial(layer_kernel, blocks, tiles),
-        out_shape=jax.ShapeDtypeStruct(latent_video.shape, bf16),
+        out_shape=pltpu.VMEM(latent_video.shape, bf16),
         in_specs=[pl.BlockSpec(memory_space=pl.ANY)] * 5,
-        out_specs=pl.BlockSpec(memory_space=pl.ANY),
+        out_specs=pl.BlockSpec(memory_space=pltpu.VMEM),
         scratch_shapes=[
             pltpu.VMEM((frames, half + 4, width, cin), bf16),
             pltpu.VMEM((frames, half + 4, width, 3 * cin), bf16),
@@ -356,6 +440,9 @@
             pltpu.VMEM((1, cin), f32),
             pltpu.VMEM((chunks, flat, state), bf16),
             pltpu.VMEM((chunks, flat, state), bf16),
+            pltpu.VMEM((8, state), f32),
+            pltpu.VMEM((8, state), f32),
+            pltpu.VMEM((chunks, flat, state), bf16),
             pltpu.VMEM((frames, half, width, cin), bf16),
             dma((4,)),
             dma((9,)),
@@ -363,6 +450,10 @@
             dma,
             dma((2,)),
             dma((2,)),
+            dma,
+            dma,
+            dma((chunks,)),
+            dma((chunks,)),
             dma((chunks,)),
             dma((chunks,)),
             dma((chunks,)),
@@ -370,7 +461,7 @@
             dma((chunks,)),
         ],
         compiler_params=pltpu.CompilerParams(
-            collective_id=0, has_side_effects=True, vmem_limit_bytes=64 * 1024 * 1024
+            collective_id=0, has_side_effects=True, vmem_limit_bytes=62 * 1024 * 1024
         ),
         cost_estimate=pl.CostEstimate(
             flops=4 * pixels * 9 * cin * state, bytes_accessed=8 * pixels * cin, transcendentals=0

time: 32.6 us -> 28.3 us (0.87)
  the two profiles are of different devices: /device:TPU:7 before, /device:TPU:5 now
where the time goes in v2:
time: 28.3 us; the launch traced here: 28.1 us
  Pallas kernels  27 us (95%)
  local copies, waits for them, and re-layouts  1.15 us (4%)
    pallas_call x1, Pallas kernels, on_device(): pl.pallas_call(functools.partial(layer_kernel, blocks, tiles), out_shape=...  27 us
    unnamed x1, local copies, waits for them, and re-layouts  1.15 us

profile of v2, /device:TPU:5, one launch (start us, length us, event | category | flops | bytes accessed | tf_op | source)
XLA Modules:
  0.0 28.1 jit_solution(18220551636074755064)
XLA Ops:
  0.0 27.0 %shard_map.55 = bf16[6,32,32,128]{3,2,1,0:T(8,128)(2,1)S(1)} custom-call(bf16[6,32,32,128]{3,2,1,0:T(8,128)(2,1)} %x_ref.1, bf16[1152,256]{1,0:T(8,128)(2,1)} %bitcast.2, bf16[3,3,256,128]{3,2,1,0:T(8,128)(2,1)} %w2_ref.1, f32[6,256]{1,0:T(8,128)} %decay_ref.1, f32[1,128]{1,0:T(1,128)} %bitcast.3), custom_call_target="tpu_custom_call" | custom-call | flops 7247757312 | bytes 6291456 | tf_op jit(solution)/shard_map/pallas_call | solution.py:427
  27.0 1.1 %copy.7 = bf16[6,32,32,128]{3,2,1,0:T(8,128)(2,1)} copy(bf16[6,32,32,128]{3,2,1,0:T(8,128)(2,1)S(1)} %shard_map.55) | data formatting | bytes 3145728

commit v3 on v2

--- a/solution.py
+++ b/solution.py
@@ -9,7 +9,7 @@
 
 MESH = pl.DeviceIdType.MESH
 STEP = 2
-LAG = 3
+LAG = 2
 
 
 def layer_kernel(
@@ -109,15 +109,25 @@
     )
     pl.semaphore_wait(barrier, expected)
 
-    side = pltpu.make_async_remote_copy(
-        src_ref=x_ref.at[:, pl.ds((half - 2) * o, half + 2)],
-        dst_ref=xp.at[:, pl.ds(2 * c, half + 2), own_cols],
-        send_sem=side_send,
-        recv_sem=side_recv,
-        device_id=(t, z, o),
-        device_id_type=MESH,
-    )
-    side.start()
+    def side_copy(k, rows, core, columns_at):
+        start = half * (1 - core) if rows == 2 * STEP else jnp.where(
+            core == 0, half - STEP * k, STEP * k + 2
+        )
+        sent = start - 2 + half * core
+        return pltpu.make_async_remote_copy(
+            src_ref=x_ref.at[:, pl.ds(sent, rows)],
+            dst_ref=xp.at[:, pl.ds(start, rows), columns_at],
+            send_sem=side_send.at[k],
+            recv_sem=side_recv.at[k],
+            device_id=(t, z, o),
+            device_id_type=MESH,
+        )
+
+    sides = [
+        side_copy(k, 2 * STEP if k == 0 else STEP, o, own_cols) for k in range(chunks - 1)
+    ]
+    for copy in sides:
+        copy.start()
 
     def to_down():
         return pltpu.make_async_remote_copy(
@@ -170,15 +180,6 @@
     @pl.when(sends_pair)
     def _():
         decay_copy().start()
-
-    pltpu.make_async_remote_copy(
-        src_ref=x_ref.at[:, pl.ds((half - 2) * o, half + 2)],
-        dst_ref=xp.at[:, pl.ds(2 * o, half + 2), other_cols],
-        send_sem=side_send,
-        recv_sem=side_recv,
-        device_id=(t, z, o),
-        device_id_type=MESH,
-    ).wait_recv()
 
     def columns(rows):
         return lax.rem(lax.broadcasted_iota(jnp.int32, (rows, 128), 0), width)
@@ -197,7 +198,12 @@
     def drive_chunk(k):
         @pl.when(k == 0)
         def _():
+            side_copy(k, 2 * STEP, c, other_cols).wait_recv()
             spread((half + 2) * o)
+
+        @pl.when((k > 0) & (k < chunks - 1))
+        def _():
+            side_copy(k, STEP, c, other_cols).wait_recv()
 
         @pl.when(k == chunks - 1)
         def _():
@@ -369,7 +375,8 @@
 
     lax.fori_loop(0, 2 * chunks, turn, 0)
 
-    side.wait_send()
+    for copy in sides:
+        copy.wait_send()
 
     @pl.when(sends_pair)
     def _():
@@ -446,8 +453,8 @@
             pltpu.VMEM((frames, half, width, cin), bf16),
             dma((4,)),
             dma((9,)),
-            dma,
-            dma,
+            dma((chunks - 1,)),
+            dma((chunks - 1,)),
             dma((2,)),
             dma((2,)),
             dma,

time: 28.3 us -> 27.4 us (0.968)
  Pallas kernels: 27 us -> 26.1 us
    pallas_call x1, Pallas kernels: 27 us -> 26.1 us  [on_device(): pl.pallas_call(functools.partial(layer_kernel, blocks, tiles), out_shape=...]
where the time goes in v3:
time: 27.4 us; the launch traced here: 27.3 us
  Pallas kernels  26.1 us (95%)
  local copies, waits for them, and re-layouts  1.15 us (4%)
    pallas_call x1, Pallas kernels, on_device(): pl.pallas_call(functools.partial(layer_kernel, blocks, tiles), out_shape=...  26.1 us
    unnamed x1, local copies, waits for them, and re-layouts  1.15 us

profile of v3, /device:TPU:5, one launch (start us, length us, event | category | flops | bytes accessed | tf_op | source)
XLA Modules:
  0.0 27.3 jit_solution(630688851220287887)
XLA Ops:
  0.0 26.1 %shard_map.55 = bf16[6,32,32,128]{3,2,1,0:T(8,128)(2,1)S(1)} custom-call(bf16[6,32,32,128]{3,2,1,0:T(8,128)(2,1)} %x_ref.1, bf16[1152,256]{1,0:T(8,128)(2,1)} %bitcast.2, bf16[3,3,256,128]{3,2,1,0:T(8,128)(2,1)} %w2_ref.1, f32[6,256]{1,0:T(8,128)} %decay_ref.1, f32[1,128]{1,0:T(1,128)} %bitcast.3), custom_call_target="tpu_custom_call" | custom-call | flops 7247757312 | bytes 6291456 | tf_op jit(solution)/shard_map/pallas_call | solution.py:434
  26.1 1.1 %copy.7 = bf16[6,32,32,128]{3,2,1,0:T(8,128)(2,1)} copy(bf16[6,32,32,128]{3,2,1,0:T(8,128)(2,1)S(1)} %shard_map.55) | data formatting | bytes 3145728
